TPU v7x, 768 devices: a whole 4x8x12 slice. The times are simulated.
768 devices in a mesh: wide: 48 (over z_lo, y), grp: 16 (over z_hi, x, core).
Axes of the slice: x: 4, y: 8, z: 12 (z_hi: 2, z_lo: 6; z = z_hi * 6 + z_lo), core: 2. Of those that a mesh axis runs over, the one named last changes fastest.
Arguments:
- pooled: bfloat16 [6144, 49152], P(None, ('wide', 'grp')), may hold values from -6 to 6
- owner_order: int32 [256], replicated, may hold values from 0 to 255, each once
- fm_proj: bfloat16 [2, 256, 32], replicated, may hold values from -0.375 to 0.375
- fm_mix: bfloat16 [2, 128, 256], replicated, may hold values from -0.375 to 0.375
- fm_out: bfloat16 [2, 32, 192], replicated, may hold values from -0.078125 to 0.078125
- lcb_weight: bfloat16 [2, 128, 256], replicated, may hold values from -0.375 to 0.375
- gain: float32 [2, 192], replicated, may hold values from 0.5 to 1.5
- cotangent: bfloat16 [6144, 49152], P(('wide', 'grp')), may hold values from -6 to 6
Outputs:
- layer_out: bfloat16 [6144, 49152], P(('wide', 'grp'))
- d_pooled: bfloat16 [6144, 49152], P(None, ('wide', 'grp'))
- grad_fm_proj: float32 [2, 256, 32], replicated
- grad_fm_mix: float32 [2, 128, 256], replicated
- grad_fm_out: float32 [2, 32, 192], replicated
- grad_lcb: float32 [2, 128, 256], replicated
- grad_gain: float32 [2, 192], replicated
Inputs may be any that keep to these rules, and one draw needn't show every extreme that they name: `owner_order`: each feature stands in exactly one slot.
All inputs are finite; a program needn't handle non-finite values.
Results may differ from a plain program's by a relative error of at most 0.019.
Values may be sent and summed in bfloat16 or wider, within the bound.
A program may use at most 32 MiB of HBM per device.

v0:
```python
import jax
import jax.numpy as jnp
from jax import lax
from jax.sharding import PartitionSpec as P

F = 256
E = 192


def product(form, left, right):
    return jnp.einsum(form, left, right, preferred_element_type=jnp.float32)


def layer_forward(embeds, fm_proj, fm_mix, fm_out, lcb_weight, gain):
    proj_z = product("nfe,fk->nek", embeds, fm_proj).astype(jnp.bfloat16)
    inter_m = product("nfe,nek->nfk", embeds, proj_z).astype(jnp.bfloat16)
    mix_q = product("gf,nfk->ngk", fm_mix, inter_m).astype(jnp.bfloat16)
    fm_branch = product("ngk,ke->nge", mix_q, fm_out)
    lcb_branch = product("lf,nfe->nle", lcb_weight, embeds)
    summed = jnp.concatenate([fm_branch, lcb_branch], axis=1) + embeds.astype(jnp.float32)
    center = summed - jnp.mean(summed, axis=-1, keepdims=True)
    variance = jnp.mean(center * center, axis=-1, keepdims=True)
    inv_std = lax.rsqrt(variance + 1e-05)
    normed = center * inv_std
    result = (normed * gain).astype(jnp.bfloat16)
    return (result, (proj_z, inter_m, mix_q, normed, inv_std))


def layer_backward(embeds, cot_rows, saved, fm_proj, fm_mix, fm_out, lcb_weight, gain):
    proj_z, inter_m, mix_q, normed, inv_std = saved
    split = fm_mix.shape[0]
    cot_float = cot_rows.astype(jnp.float32)
    grad_gain = jnp.sum(cot_float * normed, axis=(0, 1))
    d_norm = cot_float * gain
    grad_sum = inv_std * (
        d_norm
        - jnp.mean(d_norm, axis=-1, keepdims=True)
        - normed * jnp.mean(d_norm * normed, axis=-1, keepdims=True)
    )
    grad_sum = grad_sum.astype(jnp.bfloat16)
    d_fm_rows = grad_sum[:, :split]
    d_lcb_rows = grad_sum[:, split:]
    grad_lcb = product("nle,nfe->lf", d_lcb_rows, embeds)
    grad_fm_out = product("ngk,nge->ke", mix_q, d_fm_rows)
    grad_mix_q = product("nge,ke->ngk", d_fm_rows, fm_out).astype(jnp.bfloat16)
    grad_fm_mix = product("ngk,nfk->gf", grad_mix_q, inter_m)
    grad_inter = product("gf,ngk->nfk", fm_mix, grad_mix_q).astype(jnp.bfloat16)
    grad_proj_z = product("nfe,nfk->nek", embeds, grad_inter).astype(jnp.bfloat16)
    grad_fm_proj = product("nfe,nek->fk", embeds, grad_proj_z)
    grad_embeds = (
        grad_sum.astype(jnp.float32)
        + product("lf,nle->nfe", lcb_weight, d_lcb_rows)
        + product("nfk,nek->nfe", grad_inter, proj_z)
        + product("fk,nek->nfe", fm_proj, grad_proj_z)
    ).astype(jnp.bfloat16)
    return (grad_embeds, (grad_fm_proj, grad_fm_mix, grad_fm_out, grad_lcb, grad_gain))


def run_layers(embeds, cot_rows, fm_proj, fm_mix, fm_out, lcb_weight, gain):
    depth = fm_proj.shape[0]
    inputs = []
    saves = []
    current = embeds
    for layer in range(depth):
        inputs.append(current)
        current, saved = layer_forward(
            current, fm_proj[layer], fm_mix[layer], fm_out[layer], lcb_weight[layer], gain[layer]
        )
        saves.append(saved)
    back = cot_rows
    grad_list = [None] * depth
    for layer in reversed(range(depth)):
        back, grads = layer_backward(
            inputs[layer],
            back,
            saves[layer],
            fm_proj[layer],
            fm_mix[layer],
            fm_out[layer],
            lcb_weight[layer],
            gain[layer],
        )
        grad_list[layer] = grads
    stacked = tuple((jnp.stack([entry[which] for entry in grad_list]) for which in range(5)))
    return (current, back, stacked)


def shards(pooled, owner_order, fm_proj, fm_mix, fm_out, lcb_weight, gain, cotangent):
    wide_size = lax.axis_size("wide")
    group_size = lax.axis_size("grp")
    samples_all, piece_cols = pooled.shape
    row_count = cotangent.shape[0]
    arranged = pooled.reshape(wide_size, group_size, row_count, piece_cols)
    arranged = arranged.transpose(1, 0, 2, 3).reshape(samples_all, piece_cols)
    sectioned = lax.all_to_all(arranged, "grp", split_axis=0, concat_axis=1, tiled=True)
    received = lax.all_to_all(sectioned, "wide", split_axis=0, concat_axis=1, tiled=True)
    position = jnp.zeros((F,), jnp.int32).at[owner_order].set(jnp.arange(F, dtype=jnp.int32))
    embeds = jnp.take(received.reshape(row_count, F, E), position, axis=1)
    cot_rows = cotangent.reshape(row_count, F, E)
    result, grad_embeds, grads = run_layers(
        embeds, cot_rows, fm_proj, fm_mix, fm_out, lcb_weight, gain
    )
    layer_out = result.reshape(row_count, F * E)
    back_rows = jnp.take(grad_embeds, owner_order, axis=1).reshape(row_count, F * E)
    across = lax.all_to_all(back_rows, "wide", split_axis=1, concat_axis=0, tiled=True)
    grouped = lax.all_to_all(across, "grp", split_axis=1, concat_axis=0, tiled=True)
    d_pooled = grouped.reshape(group_size, wide_size, row_count, piece_cols)
    d_pooled = d_pooled.transpose(1, 0, 2, 3).reshape(samples_all, piece_cols)
    totals = lax.psum(grads, ("wide", "grp"))
    scale = 1.0 / samples_all
    return (
        layer_out,
        d_pooled,
        totals[0] * scale,
        totals[1] * scale,
        totals[2] * scale,
        totals[3] * scale,
        totals[4] * scale,
    )


def solution(mesh):
    return jax.shard_map(
        shards,
        mesh=mesh,
        in_specs=(P(None, ("wide", "grp")), P(), P(), P(), P(), P(), P(), P(("wide", "grp"), None)),
        out_specs=(P(("wide", "grp"), None), P(None, ("wide", "grp")), P(), P(), P(), P(), P()),
        check_vma=False,
    )
```

profile of v0, /device:TPU:1, one launch (start us, length us, event | category | flops | bytes accessed | tf_op | source)
XLA Modules:
  0.0 697.1 jit_solution(8505140150063691112)
XLA Ops:
  7.2 1.8 copy.30
  10.1 38.3 %all_to_all.64 = bf16[16,384,64]{1,2,0:T(8,128)(2,1)S(1)} all-to-all(bf16[16,384,64]{1,2,0:T(8,128)(2,1)S(1)} %copy.32), channel_id=1, replica_groups=mesh['wide'=48,'grp'=16] {'grp'}, dimensions={0} | all-to-all | bytes 1572864 | tf_op jit(solution)/shard_map/all_to_all | solution.py:95
  49.7 1.9 all_to_all.51
  51.6 28.2 %all-to-all-start.1 = ((bf16[48,8,1024]{2,1,0:T(8,128)(2,1)}), bf16[48,8,1024]{2,1,0:T(8,128)(2,1)S(1)}, u32[]{:S(2)}, u32[]{:S(2)}) async-start(bf16[48,8,1024]{2,1,0:T(8,128)(2,1)} %all_to_all.51), calls=%async_computation.1 | async-start | bytes 1572864 | tf_op jit(solution)/shard_map/all_to_all | solution.py:96
  79.8 2.4 reshape.104
  82.2 1.9 copy.38
  86.4 23.0 %all-to-all-done.1 = bf16[48,8,1024]{2,1,0:T(8,128)(2,1)S(1)} async-done(((bf16[48,8,1024]{2,1,0:T(8,128)(2,1)}), bf16[48,8,1024]{2,1,0:T(8,128)(2,1)S(1)}, u32[]{:S(2)}, u32[]{:S(2)}) %all-to-all-start.1) | async-done | bytes 786464 | tf_op jit(solution)/shard_map/all_to_all | solution.py:96
  110.7 2.2 reshape.100
  114.4 3.0 gather_fusion
  117.4 1.9 copy.36
  133.7 2.6 copy.39
  136.3 3.0 gather_fusion.1
  139.3 2.0 select_bitcast_fusion
  142.5 3.3 all_to_all.54
  145.8 2.5 copy.41
  148.2 9.5 %all-to-all-start.2 = ((bf16[8,48,1024]{2,0,1:T(8,128)(2,1)}), bf16[8,48,1024]{2,0,1:T(8,128)(2,1)}, u32[]{:S(2)}, u32[]{:S(2)}) async-start(bf16[8,48,1024]{2,0,1:T(8,128)(2,1)} %copy.41), calls=%async_computation.2 | async-start | bytes 1572864 | tf_op jit(solution)/shard_map/all_to_all | solution.py:105
  161.3 23.7 %all-to-all-done.2 = bf16[8,48,1024]{2,0,1:T(8,128)(2,1)} async-done(((bf16[8,48,1024]{2,0,1:T(8,128)(2,1)}), bf16[8,48,1024]{2,0,1:T(8,128)(2,1)}, u32[]{:S(2)}, u32[]{:S(2)}) %all-to-all-start.2) | async-done | bytes 786464 | tf_op jit(solution)/shard_map/all_to_all | solution.py:105
  185.1 3.2 all_to_all.57
  188.2 2.7 copy.42
  191.0 10.4 %all-to-all-start.3 = ((bf16[384,16,64]{0,2,1:T(8,128)(2,1)}), bf16[384,16,64]{0,2,1:T(8,128)(2,1)S(1)}, u32[]{:S(2)}, u32[]{:S(2)}) async-start(bf16[384,16,64]{0,2,1:T(8,128)(2,1)} %copy.42), calls=%async_computation.3 | async-start | bytes 1572864 | tf_op jit(solution)/shard_map/all_to_all | solution.py:106
  203.0 111.2 %all-reduce = (f32[2,32,192]{2,1,0:T(8,128)S(1)}, f32[2,192]{1,0:T(2,128)S(1)}) all-reduce(f32[2,32,192]{2,1,0:T(8,128)S(1)} %pad_maximum_fusion.3, f32[2,192]{1,0:T(2,128)S(1)} %pad_maximum_fusion.4), channel_id=1, replica_groups=mesh['wide'=48,'grp'=16] {'wide','grp'}, use_global_device_ids=true, to_apply=%region_11.13 | all-reduce | flops 12672 | bytes 101376 | tf_op jit(solution)/shard_map/psum | solution.py:109
  316.2 2.0 reshape.101
  318.8 363.8 %all-reduce.4.cloned.1.call-done = (f32[2,256,32]{1,2,0:T(8,128)}, f32[2,128,256]{2,1,0:T(8,128)}, f32[2,128,256]{2,1,0:T(8,128)}) async-done(((f32[2,256,32]{1,2,0:T(8,128)}, f32[2,128,256]{2,1,0:T(8,128)}, f32[2,128,256]{2,1,0:T(8,128)}), (f32[2,256,32]{1,2,0:T(8,128)}, f32[2,128,256]{2,1,0:T(8,128)}, f32[2,128,256]{2,1,0:T(8,128)})) %all-reduce.4.cloned.1.call-update) | async-done | bytes 589840 | tf_op jit(solution)/shard_map/psum | solution.py:109
  684.1 1.7 broadcast_multiply_fusion.1
  (118 shorter events, 36.2 us)
Async XLA Ops:
  49.7 30.1 %copy-start.2 = (bf16[8,49152]{1,0:T(8,128)(2,1)S(1)}, bf16[8,49152]{1,0:T(8,128)(2,1)}, u32[]{:S(2)}) copy-start(bf16[8,49152]{1,0:T(8,128)(2,1)} %param.17) | copy-start | bytes 2359300
  51.6 57.8 %all-to-all-start.1 = ((bf16[48,8,1024]{2,1,0:T(8,128)(2,1)}), bf16[48,8,1024]{2,1,0:T(8,128)(2,1)S(1)}, u32[]{:S(2)}, u32[]{:S(2)}) async-start(bf16[48,8,1024]{2,1,0:T(8,128)(2,1)} %all_to_all.51), calls=%async_computation.1 | async-start | bytes 1572864 | tf_op jit(solution)/shard_map/all_to_all | solution.py:96
  82.2 1.9 copy-start.19
  82.2 4.1 copy-start.18
  86.3 35.0 %copy-start.15 = (pred[256]{0:T(512)(128)(4,1)}, pred[256]{0:T(512)(128)(4,1)S(1)}, u32[]{:S(2)}) copy-start(pred[256]{0:T(512)(128)(4,1)S(1)} %compare_and_fusion.1) | copy-start | bytes 772
  114.4 5.0 copy-start.13
  119.4 1.9 copy-start
  119.4 1.0 copy-start.7
  119.8 1.1 copy-start.10
  119.8 1.2 copy-start.12
  120.5 1.1 copy-start.8
  126.6 0.6 copy-start.3
  127.8 0.8 copy-start.14
  129.7 1.5 copy-start.1
  129.7 1.5 copy-start.16
  131.6 0.8 copy-start.11
  133.7 5.6 copy-start.20
  148.2 9.8 %copy-start.17 = (pred[256]{0:T(512)(128)(4,1)S(1)}, pred[256]{0:T(512)(128)(4,1)}, u32[]{:S(2)}) copy-start(pred[256]{0:T(512)(128)(4,1)} %copy-done.15) | copy-start | bytes 772
  148.2 36.8 %all-to-all-start.2 = ((bf16[8,48,1024]{2,0,1:T(8,128)(2,1)}), bf16[8,48,1024]{2,0,1:T(8,128)(2,1)}, u32[]{:S(2)}, u32[]{:S(2)}) async-start(bf16[8,48,1024]{2,0,1:T(8,128)(2,1)} %copy.41), calls=%async_computation.2 | async-start | bytes 1572864 | tf_op jit(solution)/shard_map/all_to_all | solution.py:105
  157.7 2.1 copy-start.4
  157.7 2.3 copy-start.6
  157.7 2.3 copy-start.9
  191.0 496.5 %all-to-all-start.3 = ((bf16[384,16,64]{0,2,1:T(8,128)(2,1)}), bf16[384,16,64]{0,2,1:T(8,128)(2,1)S(1)}, u32[]{:S(2)}, u32[]{:S(2)}) async-start(bf16[384,16,64]{0,2,1:T(8,128)(2,1)} %copy.42), calls=%async_computation.3 | async-start | bytes 1572864 | tf_op jit(solution)/shard_map/all_to_all | solution.py:106
  201.4 481.3 %all-reduce.4.cloned.1.call-start = ((), (), s32[]{:S(2)}) async-start(), calls=%async_computation.4 | async-start | bytes 1179648 | tf_op jit(solution)/shard_map/psum | solution.py:109
  (1 other events, 0.6 us)
Sparse Core Ops, SparseCore 0:
  208.8 473.7 all-reduce.3
where the time goes:
time: 698 us; the launch traced here: 697 us
  waiting for transfers between devices  411 us (59%)
  blocking collectives  149 us (21%)
  local copies, waits for them, and re-layouts  48.4 us (7%)
  starting transfers between devices  48.1 us (7%)
  other arithmetic  14.7 us (2%)
  between operations  14.7 us (2%)
  matrix products  11.1 us (2%)
    psum x1, waiting for transfers between devices, shards(): totals = lax.psum(grads, ('wide', 'grp'))  364 us
    psum x1, blocking collectives, shards(): totals = lax.psum(grads, ('wide', 'grp'))  111 us
    all_to_all x1, blocking collectives, shards(): lax.all_to_all(arranged, 'grp', split_axis=0, concat_axis=1, tiled=True)  38.3 us
    all_to_all x1, starting transfers between devices, shards(): lax.all_to_all(sectioned, 'wide', split_axis=0, concat_axis=1, tiled=True)  28.2 us
    all_to_all x1, waiting for transfers between devices, shards(): lax.all_to_all(back_rows, 'wide', split_axis=1, concat_axis=0, tiled=True)  23.7 us
    all_to_all x1, waiting for transfers between devices, shards(): lax.all_to_all(sectioned, 'wide', split_axis=0, concat_axis=1, tiled=True)  23 us
  transfers between devices with their start and end apart: 4, of which 3 were waited for; matrix products, arithmetic and copies ran while one was open for 3% of the time, Pallas kernels for 0%

commit v1 on v0

v1 whole, which is shorter than its diff:
```python
import functools

import jax
import jax.numpy as jnp
from jax import lax
from jax.experimental import pallas as pl
from jax.experimental.pallas import tpu as pltpu
from jax.sharding import PartitionSpec as P

F = 256
E = 192
MESH = pl.DeviceIdType.MESH
BF16 = jnp.bfloat16
F32 = jnp.float32


class Torus:
    def __init__(self, z_lo, y, z_hi, x):
        self.z_lo, self.y, self.z_hi, self.x = z_lo, y, z_hi, x
        self.z = z_lo * z_hi
        self.flat = y * x
        self.offsets = sorted(range(y), key=lambda o: -min(o, y - o))

    def place(self):
        wide, grp = lax.axis_index("wide"), lax.axis_index("grp")
        z_lo, y = wide // self.y, wide % self.y
        z_hi, rest = grp // (2 * self.x), grp % (2 * self.x)
        return z_hi * self.z_lo + z_lo, y, rest // 2, rest % 2

    def device(self, z, y, x, core):
        z_lo, z_hi = z % self.z_lo, z // self.z_lo
        return (z_lo * self.y + y, z_hi * 2 * self.x + x * 2 + core)

    def z_peer(self, z, j):
        step = (j // 2 + 1) * (1 - 2 * (j % 2))
        return (z + step + self.z) % self.z

    def flat_peer(self, y, x, j):
        spot = (y * self.x + x + 1 + j) % self.flat
        return spot // self.x, spot % self.x


def greet(torus):
    z, y, x, core = torus.place()
    barrier = pltpu.get_barrier_semaphore()

    def hello(where):
        pl.semaphore_signal(barrier, inc=1, device_id=where, device_id_type=MESH)

    hello(torus.device(z, y, x, 1 - core))

    def along_z(j, _):
        hello(torus.device(torus.z_peer(z, j), y, x, core))
        return 0

    def along_flat(j, _):
        y_to, x_to = torus.flat_peer(y, x, j)
        hello(torus.device(z, y_to, x_to, core))
        return 0

    lax.fori_loop(0, torus.z - 1, along_z, 0)
    lax.fori_loop(0, torus.flat - 1, along_flat, 0)
    pl.semaphore_wait(barrier, torus.z + torus.flat - 1)


def remote(src, dst, send, recv, where):
    return pltpu.make_async_remote_copy(
        src_ref=src, dst_ref=dst, send_sem=send, recv_sem=recv, device_id=where, device_id_type=MESH
    )


def take(ref, sem):
    pltpu.make_async_copy(ref, ref, sem).wait()


def send_z(torus, i, src, middle, z_send, z_recv):
    z, y, x, core = torus.place()
    y_to = (y + torus.offsets[i]) % torus.y
    landing = middle.at[z % torus.z_lo, z // torus.z_lo, y_to]
    pltpu.make_async_copy(src.at[z % torus.z_lo, y_to, z // torus.z_lo], landing, z_recv.at[i]).start()

    def step(j, _):
        z_to = torus.z_peer(z, j)
        block = src.at[z_to % torus.z_lo, y_to, z_to // torus.z_lo]
        remote(block, landing, z_send, z_recv.at[i], torus.device(z_to, y, x, core)).start()
        return 0

    lax.fori_loop(0, torus.z - 1, step, 0)


def send_flat(torus, i, middle, out, f_send, f_recv, z_recv):
    z, y, x, core = torus.place()
    y_to = (y + torus.offsets[i]) % torus.y
    take(middle.at[:, :, y_to], z_recv.at[i])
    for dx in range(torus.x):
        x_to = (x + dx) % torus.x
        block = middle.at[:, :, y_to, x_to]
        if torus.offsets[i] == 0 and dx == 0:
            pltpu.make_async_copy(block, out(y, x), f_recv.at[i]).start()
        else:
            remote(block, out(y, x), f_send, f_recv.at[i], torus.device(z, y_to, x_to, core)).start()


def take_sent(torus, spare, z_send, f_send):
    take(spare.at[pl.ds(0, (torus.z - 1) * torus.y * torus.x)], z_send)
    take(spare.at[pl.ds(0, (torus.flat - 1) * torus.z)], f_send)


def forward_kernel(torus, p_ref, r_ref, inbox, src, middle, spare, c_send, c_recv, z_send, z_recv, f_send, f_recv):
    z, y, x, core = torus.place()
    greet(torus)
    mate = torus.device(z, y, x, 1 - core)
    swaps = []
    for i in range(torus.y):
        y_to = (y + torus.offsets[i]) % torus.y
        swap = remote(
            p_ref.at[:, y_to, :, :, 1 - core], inbox.at[:, y_to], c_send.at[i], c_recv.at[i], mate
        )
        swap.start()
        swaps.append(swap)
    lanes = lax.broadcasted_iota(jnp.int32, (torus.x, 8, 128), 2)
    mine = (lanes // 64) == core
    for i in range(torus.y):
        y_to = (y + torus.offsets[i]) % torus.y
        swaps[i].wait_recv()

        def merge(k, _):
            z_lo, z_hi = k // torus.z_hi, k % torus.z_hi
            own = p_ref[z_lo, y_to, z_hi, :, core].astype(F32)
            other = inbox[z_lo, y_to, z_hi].astype(F32)
            src[z_lo, y_to, z_hi] = jnp.where(mine, own, other).astype(BF16)
            return 0

        lax.fori_loop(0, torus.z, merge, 0)
        send_z(torus, i, src, middle, z_send, z_recv)
    for i in range(torus.y):
        send_flat(torus, i, middle, lambda y, x: r_ref.at[:, y, :, x], f_send, f_recv, z_recv)
    for i in range(torus.y):
        y_from = (y - torus.offsets[i] + torus.y) % torus.y
        take(r_ref.at[:, y_from], f_recv.at[i])
    for i in range(torus.y):
        swaps[i].wait_send()
    take_sent(torus, spare, z_send, f_send)


def spare_shape(torus):
    return pltpu.VMEM((max((torus.z - 1) * torus.y * torus.x, (torus.flat - 1) * torus.z), 8, 128), BF16)


def forward_exchange(torus, pooled):
    doubled = jnp.concatenate([pooled, pooled], axis=1)
    doubled = doubled.reshape(torus.z_lo, torus.y, torus.z_hi, torus.x, 2, 8, 128)
    shape = (torus.z_lo, torus.y, torus.z_hi, torus.x, 8, 128)
    middle = (torus.z_lo, torus.z_hi, torus.y, torus.x, 8, 128)
    dma = pltpu.SemaphoreType.DMA
    landed = pl.pallas_call(
        functools.partial(forward_kernel, torus),
        out_shape=jax.ShapeDtypeStruct(shape, BF16),
        in_specs=[pl.BlockSpec(memory_space=pltpu.VMEM)],
        out_specs=pl.BlockSpec(memory_space=pltpu.VMEM),
        scratch_shapes=[
            pltpu.VMEM(shape, BF16),
            pltpu.VMEM(shape, BF16),
            pltpu.VMEM(middle, BF16),
            spare_shape(torus),
            dma((torus.y,)),
            dma((torus.y,)),
            dma,
            dma((torus.y,)),
            dma,
            dma((torus.y,)),
        ],
        compiler_params=pltpu.CompilerParams(
            collective_id=0, has_side_effects=True, vmem_limit_bytes=40 * 1024 * 1024
        ),
        name="forward_exchange",
    )(doubled)
    chips = torus.z * torus.flat
    return landed.reshape(chips, 8, 128).transpose(1, 0, 2).reshape(8, chips * 128)


def backward_kernel(
    torus, b_ref, g_ref, d_ref, t_ref, middle, spare, g_spare, g_inbox, g_half, g_parts, g_own, g_rings, g_done, g_full,
    c_send, c_recv, z_send, z_recv, f_send, f_recv,
    a_send, a_recv, s_send, s_recv, k_send, k_recv, w_send, w_recv, e_send, e_recv,
):
    z, y, x, core = torus.place()
    greet(torus)
    mate = torus.device(z, y, x, 1 - core)
    z_lo, z_hi = z % torus.z_lo, z // torus.z_lo

    first = remote(g_ref.at[1 - core], g_inbox, a_send, a_recv, mate)
    first.start()
    for i in range(torus.y):
        send_z(torus, i, b_ref, middle, z_send, z_recv)

    def to_flat(block, landing, send, recv):
        def step(j, _):
            y_to, x_to = torus.flat_peer(y, x, j)
            remote(block(y_to, x_to), landing, send, recv, torus.device(z, y_to, x_to, core)).start()
            return 0

        pltpu.make_async_copy(block(y, x), landing, recv).start()
        lax.fori_loop(0, torus.flat - 1, step, 0)

    def sum_pair():
        first.wait_recv()

        def add(k, _):
            own = g_ref[core, k].astype(F32)
            g_half[k] = (own + g_inbox[k].astype(F32)).astype(BF16)
            return 0

        lax.fori_loop(0, torus.y, add, 0)
        to_flat(lambda y_to, x_to: g_half.at[y_to, x_to], g_parts.at[y, x], s_send, s_recv)

    def sum_flat():
        take(g_parts, s_recv)

        def add(k, total):
            return total + jnp.sum(g_parts[k].astype(F32), axis=0)

        g_own[...] = lax.fori_loop(0, torus.y, add, jnp.zeros((16, 256), F32)).astype(BF16)
        landing = g_rings.at[z]
        pltpu.make_async_copy(g_own, landing, k_recv).start()

        def step(j, _):
            z_to = torus.z_peer(z, j)
            remote(g_own, landing, k_send, k_recv, torus.device(z_to, y, x, core)).start()
            return 0

        lax.fori_loop(0, torus.z - 1, step, 0)

    def sum_ring():
        take(g_rings, k_recv)

        def add(k, total):
            return total + g_rings[k].astype(F32)

        g_done[...] = lax.fori_loop(0, torus.z, add, jnp.zeros((16, 256), F32)).astype(BF16)
        to_flat(lambda y_to, x_to: g_done, g_full.at[y, x], w_send, w_recv)

    last = remote(g_full, t_ref.at[core], e_send, e_recv, mate)

    def share_pair():
        take(g_full, w_recv)
        last.start()
        t_ref[core] = g_full[...]

    between = {0: sum_pair, 2: sum_flat, 4: sum_ring, 6: share_pair}
    if torus.y < 8:
        between = {}
    swaps = []
    for i in range(torus.y):
        if i in between:
            between[i]()
        send_flat(torus, i, middle, lambda y, x: d_ref.at[:, y, :, x, core], f_send, f_recv, z_recv)
    if not between:
        for part in (sum_pair, sum_flat, sum_ring, share_pair):
            part()
    for i in range(torus.y):
        y_from = (y - torus.offsets[i] + torus.y) % torus.y
        block = d_ref.at[:, y_from, :, :, core]
        take(block, f_recv.at[i])
        swap = remote(block, block, c_send.at[i], c_recv.at[i], mate)
        swap.start()
        swaps.append(swap)
    last.wait()
    for swap in swaps:
        swap.wait()
    first.wait_send()
    take_sent(torus, spare, z_send, f_send)
    take(g_spare.at[pl.ds(0, torus.flat - 1)], s_send)
    take(g_spare.at[pl.ds(0, torus.flat - 1)], w_send)
    take(g_spare.at[pl.ds(0, torus.z - 1)], k_send)


def backward_exchange(torus, rows, grads):
    chips = torus.z * torus.flat
    blocks = rows.reshape(8, chips, 128).transpose(1, 0, 2)
    blocks = blocks.reshape(torus.z_lo, torus.y, torus.z_hi, torus.x, 8, 128)
    middle = (torus.z_lo, torus.z_hi, torus.y, torus.x, 8, 128)
    half = (torus.y, torus.x, 16, 256)
    dma = pltpu.SemaphoreType.DMA
    d_full, total = pl.pallas_call(
        functools.partial(backward_kernel, torus),
        out_shape=(
            jax.ShapeDtypeStruct((torus.z_lo, torus.y, torus.z_hi, torus.x, 2, 8, 128), BF16),
            jax.ShapeDtypeStruct((2,) + half, BF16),
        ),
        in_specs=[pl.BlockSpec(memory_space=pltpu.VMEM)] * 2,
        out_specs=[pl.BlockSpec(memory_space=pltpu.VMEM)] * 2,
        scratch_shapes=[
            pltpu.VMEM(middle, BF16),
            spare_shape(torus),
            pltpu.VMEM((max(torus.flat, torus.z) - 1, 16, 256), BF16),
            pltpu.VMEM(half, BF16),
            pltpu.VMEM(half, BF16),
            pltpu.VMEM(half, BF16),
            pltpu.VMEM((16, 256), BF16),
            pltpu.VMEM((torus.z, 16, 256), BF16),
            pltpu.VMEM((16, 256), BF16),
            pltpu.VMEM(half, BF16),
            dma((torus.y,)),
            dma((torus.y,)),
            dma,
            dma((torus.y,)),
            dma,
            dma((torus.y,)),
        ]
        + [dma] * 10,
        compiler_params=pltpu.CompilerParams(
            collective_id=1, has_side_effects=True, vmem_limit_bytes=40 * 1024 * 1024
        ),
        name="backward_exchange",
    )(blocks, grads)
    core = lax.axis_index("grp") % 2
    wide = d_full.reshape(chips * 16, 128)
    d_pooled = lax.dynamic_slice(wide, (0, core * 64), (chips * 16, 64))
    return d_pooled, total


def product(form, left, right):
    return jnp.einsum(form, left, right, preferred_element_type=F32)


def layer_forward(embeds, fm_proj, fm_mix, fm_out, lcb_weight, gain):
    proj_z = product("nfe,fk->nek", embeds, fm_proj).astype(BF16)
    inter_m = product("nfe,nek->nfk", embeds, proj_z).astype(BF16)
    mix_q = product("gf,nfk->ngk", fm_mix, inter_m).astype(BF16)
    fm_branch = product("ngk,ke->nge", mix_q, fm_out)
    lcb_branch = product("lf,nfe->nle", lcb_weight, embeds)
    summed = jnp.concatenate([fm_branch, lcb_branch], axis=1) + embeds.astype(F32)
    center = summed - jnp.mean(summed, axis=-1, keepdims=True)
    variance = jnp.mean(center * center, axis=-1, keepdims=True)
    inv_std = lax.rsqrt(variance + 1e-05)
    normed = center * inv_std
    result = (normed * gain).astype(BF16)
    return (result, (proj_z, inter_m, mix_q, normed, inv_std))


def layer_backward(embeds, cot_rows, saved, fm_proj, fm_mix, fm_out, lcb_weight, gain):
    proj_z, inter_m, mix_q, normed, inv_std = saved
    split = fm_mix.shape[0]
    cot_float = cot_rows.astype(F32)
    grad_gain = jnp.sum(cot_float * normed, axis=(0, 1))
    d_norm = cot_float * gain
    grad_sum = inv_std * (
        d_norm
        - jnp.mean(d_norm, axis=-1, keepdims=True)
        - normed * jnp.mean(d_norm * normed, axis=-1, keepdims=True)
    )
    grad_sum = grad_sum.astype(BF16)
    d_fm_rows = grad_sum[:, :split]
    d_lcb_rows = grad_sum[:, split:]
    grad_lcb = product("nle,nfe->lf", d_lcb_rows, embeds)
    grad_fm_out = product("ngk,nge->ke", mix_q, d_fm_rows)
    grad_mix_q = product("nge,ke->ngk", d_fm_rows, fm_out).astype(BF16)
    grad_fm_mix = product("ngk,nfk->gf", grad_mix_q, inter_m)
    grad_inter = product("gf,ngk->nfk", fm_mix, grad_mix_q).astype(BF16)
    grad_proj_z = product("nfe,nfk->nek", embeds, grad_inter).astype(BF16)
    grad_fm_proj = product("nfe,nek->fk", embeds, grad_proj_z)
    grad_embeds = (
        grad_sum.astype(F32)
        + product("lf,nle->nfe", lcb_weight, d_lcb_rows)
        + product("nfk,nek->nfe", grad_inter, proj_z)
        + product("fk,nek->nfe", fm_proj, grad_proj_z)
    ).astype(BF16)
    return (grad_embeds, (grad_fm_proj, grad_fm_mix, grad_fm_out, grad_lcb, grad_gain))


def run_layers(embeds, cot_rows, fm_proj, fm_mix, fm_out, lcb_weight, gain):
    depth = fm_proj.shape[0]
    inputs, saves = [], []
    current = embeds
    for layer in range(depth):
        inputs.append(current)
        current, saved = layer_forward(
            current, fm_proj[layer], fm_mix[layer], fm_out[layer], lcb_weight[layer], gain[layer]
        )
        saves.append(saved)
    back = cot_rows
    grad_list = [None] * depth
    for layer in reversed(range(depth)):
        back, grad_list[layer] = layer_backward(
            inputs[layer], back, saves[layer],
            fm_proj[layer], fm_mix[layer], fm_out[layer], lcb_weight[layer], gain[layer],
        )
    return current, back, grad_list


def pack(grads):
    proj, mix, out, lcb, gain = grads
    corner = jnp.pad(gain.reshape(3, 64), ((0, 29), (0, 0)))
    return jnp.concatenate([proj.T, mix, lcb, jnp.concatenate([out, corner], axis=1)], axis=0)


def shards(torus, pooled, owner_order, fm_proj, fm_mix, fm_out, lcb_weight, gain, cotangent):
    row_count = cotangent.shape[0]
    received = forward_exchange(torus, pooled)
    chosen = (owner_order[None, :] == jnp.arange(F, dtype=jnp.int32)[:, None]).astype(BF16)
    embeds = product("fs,nse->nfe", chosen, received.reshape(row_count, F, E)).astype(BF16)
    cot_rows = cotangent.reshape(row_count, F, E)
    result, grad_embeds, grad_list = run_layers(
        embeds, cot_rows, fm_proj, fm_mix, fm_out, lcb_weight, gain
    )
    layer_out = result.reshape(row_count, F * E)
    back_rows = product("fs,nfe->nse", chosen, grad_embeds).astype(BF16).reshape(row_count, F * E)
    packed = jnp.stack([pack(entry) for entry in grad_list]).astype(BF16)
    packed = jnp.pad(packed.reshape(2, 32, 10, 256), ((0, 0), (0, 0), (0, 6), (0, 0)))
    d_pooled, total = backward_exchange(torus, back_rows, packed.reshape(2, torus.y, torus.x, 16, 256))
    total = total.reshape(2, 32, 16, 256)[:, :, :10].reshape(2, 320, 256).astype(F32)
    total = total * (1.0 / pooled.shape[0])
    return (
        layer_out,
        d_pooled,
        total[:, :32].transpose(0, 2, 1),
        total[:, 32:160],
        total[:, 288:, :192],
        total[:, 160:288],
        total[:, 288:291, 192:].reshape(2, E),
    )


def solution(mesh):
    torus = Torus(6, mesh.shape["wide"] // 6, 2, mesh.shape["grp"] // 4)
    return jax.shard_map(
        functools.partial(shards, torus),
        mesh=mesh,
        in_specs=(P(None, ("wide", "grp")), P(), P(), P(), P(), P(), P(), P(("wide", "grp"), None)),
        out_specs=(P(("wide", "grp"), None), P(None, ("wide", "grp")), P(), P(), P(), P(), P()),
        check_vma=False,
    )
```

time: 698 us -> 173 us (0.25)
  waiting for transfers between devices: 411 us -> 0 us
  blocking collectives: 149 us -> 0 us
  Pallas kernels: 0 us -> 110 us
  starting transfers between devices: 48.1 us -> 0 us
  local copies, waits for them, and re-layouts: 48.4 us -> 32.9 us
  between operations: 14.7 us -> 1.23 us
    psum x1 -> x0, waiting for transfers between devices: 364 us -> none  [shards(): totals = lax.psum(grads, ('wide', 'grp'))]
    psum x1 -> x0, blocking collectives: 111 us -> none  [shards(): totals = lax.psum(grads, ('wide', 'grp'))]
    pallas_call x0 -> x2, Pallas kernels: none -> 110 us  [the longest x1 54.9 us: backward_exchange(): pl.pallas_call(functools.partial(backward_kernel, torus), out_shape=(jax....]
    all_to_all x3 -> x0, starting transfers between devices: 48.1 us -> none  [the longest x1 28.2 us: shards(): lax.all_to_all(sectioned, 'wide', split_axis=0, concat_axis=1, tiled=True)]
    all_to_all x3 -> x0, waiting for transfers between devices: 46.7 us -> none  [the longest x1 23.7 us: shards(): lax.all_to_all(back_rows, 'wide', split_axis=1, concat_axis=0, tiled=True)]
    all_to_all x1 -> x0, blocking collectives: 38.3 us -> none  [shards(): lax.all_to_all(arranged, 'grp', split_axis=0, concat_axis=1, tiled=True)]
    all_to_all x9 -> x0, local copies, waits for them, and re-layouts: 17.8 us -> none  [the longest x3 6.8 us: shards(): lax.all_to_all(across, 'grp', split_axis=1, concat_axis=0, tiled=True)]
    gather x3 -> x0, local copies, waits for them, and re-layouts: 7.95 us -> none  [the longest x2 4.95 us: shards(): embeds = jnp.take(received.reshape(row_count, F, E), position, axis=1)]
  transfers between devices with their start and end apart: 4 -> 0, of which waited for: 3 -> 0; matrix products, arithmetic and copies ran while one was open for 3% -> 0% of each run, Pallas kernels for 0% -> 0%
where the time goes in v1:
time: 173 us; the launch traced here: 172 us
  Pallas kernels  110 us (64%)
  local copies, waits for them, and re-layouts  32.9 us (19%)
  matrix products  14.4 us (8%)
  other arithmetic  14 us (8%)
    pallas_call x1, Pallas kernels, backward_exchange(): pl.pallas_call(functools.partial(backward_kernel, torus), out_shape=(jax....  54.9 us
    pallas_call x1, Pallas kernels, forward_exchange(): pl.pallas_call(functools.partial(forward_kernel, torus), out_shape=jax.Sh...  54.7 us
    dot_general x31, matrix products, product(): return jnp.einsum(form, left, right, preferred_element_type=F32)  14.4 us
    unnamed x70, local copies, waits for them, and re-layouts  9.22 us
    convert_element_type x2, local copies, waits for them, and re-layouts, layer_backward(): cot_float = cot_rows.astype(F32)  6.21 us
    convert_element_type x2, other arithmetic, layer_backward(): grad_sum = grad_sum.astype(BF16)  5.13 us

profile of v1, /device:TPU:1, one launch (start us, length us, event | category | flops | bytes accessed | tf_op | source)
XLA Modules:
  0.0 172.3 jit_solution(1170028404217589762)
XLA Ops:
  0.6 1.3 fusion.93
  2.0 2.7 %pad_maximum_fusion = bf16[6144,128]{0,1:T(8,128)(2,1)} fusion(bf16[6144,64]{0,1:T(8,128)(2,1)} %param.8), kind=kLoop, calls=%fused_computation.10 | loop fusion | flops 3145728 | bytes 2359296 | tf_op jit(solution)/shard_map/concatenate | solution.py:151
  4.7 1.9 %copy.31 = bf16[6144,128]{1,0:T(8,128)(2,1)S(1)} copy(bf16[6144,128]{0,1:T(8,128)(2,1)} %pad_maximum_fusion) | data formatting | bytes 3145728 | tf_op jit(solution)/shard_map/concatenate | solution.py:151
  6.6 54.7 %forward_exchange.1 = bf16[6,8,2,4,8,128]{5,4,3,2,1,0:T(8,128)(2,1)S(1)} custom-call(bf16[6,8,2,4,2,8,128]{6,5,4,3,2,1,0:T(8,128)(2,1)S(1)} %bitcast.180), custom_call_target="tpu_custom_call" | custom-call | tf_op jit(solution)/shard_map/forward_exchange/pallas_call | solution.py:156
  67.3 1.1 copy-done
  69.7 3.4 %reshape.113 = f32[8,256,192]{2,1,0:T(8,128)} reshape(bf16[8,49152]{1,0:T(8,128)(2,1)} %param.15) | data formatting | bytes 2359296 | tf_op jit(solution)/shard_map/convert_element_type | solution.py:345
  73.1 2.8 %copy.35 = f32[8,256,192]{1,2,0:T(8,128)} copy(f32[8,256,192]{2,1,0:T(8,128)} %reshape.113) | data formatting | bytes 3145728 | tf_op jit(solution)/shard_map/convert_element_type | solution.py:345
  75.9 3.3 %multiply_reduce_fusion = (bf16[192]{0:T(256)(128)(2,1)}, f32[8,256]{1,0:T(8,128)}, f32[8,256]{1,0:T(8,128)}) fusion(f32[8,256,192]{1,2,0:T(8,128)} %copy.35, f32[8,256,192]{1,2,0:T(8,128)} %copy-done, f32[8,256]{1,0:T(8,128)} %add_rsqrt_fusion, f32[8,256]{1,0:T(8,128)} %copy-done.21, f32[192]{0:T(256)} %bitcast.196), kind=kLoop, calls=%fused_computation.21 | loop fusion | flops 3141440 | bytes 3179648 | tf_op jit(solution)/shard_map/reduce_sum | solution.py:346
  79.2 1.2 reshape.108
  81.2 3.4 %multiply_convert_fusion = (bf16[8,256,192]{1,2,0:T(8,128)(2,1)S(1)}, bf16[8,256,192]{1,2,0:T(8,128)(2,1)}) fusion(f32[8,256,192]{1,2,0:T(8,128)} %copy.35, f32[8,256,192]{1,2,0:T(8,128)} %copy-done, f32[8,256]{1,0:T(8,128)S(1)} %get-tuple-element.42, f32[8,256]{1,0:T(8,128)S(1)} %get-tuple-element.43, f32[192]{0:T(256)} %bitcast.197, ...), kind=kLoop, calls=%fused_computation.22 | loop fusion | flops 3932160 | bytes 4752128 | tf_op jit(solution)/shard_map/convert_element_type | solution.py:353
  86.9 0.8 stack.10
  87.6 2.2 %copy.34 = bf16[8,256,192]{2,1,0:T(8,128)(2,1)} copy(bf16[8,256,192]{1,2,0:T(8,128)(2,1)} %get-tuple-element.36) | data formatting | bytes 1572864 | tf_op jit(solution)/shard_map/convert_element_type | solution.py:338
  89.8 3.4 %reshape.105 = bf16[8,49152]{1,0:T(8,128)(2,1)} reshape(bf16[8,256,192]{2,1,0:T(8,128)(2,1)} %copy.34) | data formatting | bytes 1572864 | tf_op jit(solution)/shard_map/reshape | solution.py:407
  94.5 1.8 %fusion.7 = (bf16[192]{0:T(256)(128)(2,1)S(1)}, f32[8,256]{1,0:T(8,128)S(1)}, f32[8,256]{1,0:T(8,128)S(1)}, bf16[8,256,192]{1,2,0:T(8,128)(2,1)}) fusion(f32[8,256,192]{1,2,0:T(8,128)S(1)} %get-tuple-element.34, f32[8,256]{1,0:T(8,128)S(1)} %add_rsqrt_fusion.1, f32[8,256]{1,0:T(8,128)S(1)} %broadcast_multiply_fusion.5, f32[192]{0:T(256)S(1)} %bitcast.194, ...), kind=kOutput, calls=%fused_computation.9 | convolution fusion | flops 30666560 | bytes 6473088 | tf_op jit(solution)/shard_map/fk,nek->nfe/dot_general | solution.py:324
  96.5 1.7 fusion.5
  101.0 1.5 fusion.33
  102.5 3.2 %fusion.12 = bf16[8,256,192]{1,2,0:T(8,128)(2,1)} fusion(f32[8,256,192]{1,2,0:T(8,128)S(1)} %fusion.95, f32[8,192,256]{2,1,0:T(8,128)} %fusion.33, bf16[8,256,192]{1,2,0:T(8,128)(2,1)S(1)} %fusion.5, bf16[8,192,32]{1,2,0:T(8,128)(2,1)S(1)} %convolution_convert_fusion.4, s32[256]{0:T(256)S(1)} %copy-done.30, bf16[2,256,32]{1,2,0:T(8,128)(2,1)S(1)} %copy-done.20), kind=kOutput, calls=%fused_computation.33 | convolution fusion | flops 228917248 | bytes 4867072 | tf_op jit(solution)/shard_map/fs,nfe->nse/dot_general | solution.py:324
  105.7 1.4 copy.36
  107.1 1.2 reshape_reshape.7
  108.9 54.9 %backward_exchange.1 = (bf16[6,8,2,4,2,8,128]{6,5,4,3,2,1,0:T(8,128)(2,1)S(1)}, bf16[2,8,4,16,256]{4,3,2,1,0:T(8,128)(2,1)S(1)}) custom-call(bf16[6,8,2,4,8,128]{5,4,3,2,1,0:T(8,128)(2,1)S(1)} %bitcast.181, bf16[2,8,4,16,256]{4,3,2,1,0:T(8,128)(2,1)S(1)} %bitcast.183), custom_call_target="tpu_custom_call" | custom-call | tf_op jit(solution)/shard_map/backward_exchange/pallas_call | solution.py:285
  163.9 1.7 constant_dynamic-slice_fusion
  165.5 2.4 %copy.47 = bf16[6144,64]{0,1:T(8,128)(2,1)} copy(bf16[6144,64]{1,0:T(8,128)(2,1)} %constant_dynamic-slice_fusion) | data formatting | bytes 1572864
  170.2 0.7 copy.45
  171.5 0.7 copy.43
  (121 shorter events, 17.3 us)
Async XLA Ops:
  2.0 62.9 %copy-start.25 = (f32[1,192]{1,0:T(1,128)}, f32[1,192]{1,0:T(1,128)S(1)}, u32[]{:S(2)}) copy-start(f32[1,192]{1,0:T(1,128)S(1)} %get-tuple-element.40) | copy-start | bytes 2308
  61.4 1.2 copy-start.18
  62.1 1.2 copy-start.11
  62.6 1.5 copy-start.8
  65.7 1.2 copy-start.26
  67.3 1.2 copy-start
  81.1 3.5 %copy-start.17 = (bf16[8,128,32]{1,2,0:T(8,128)(2,1)S(1)}, bf16[8,128,32]{1,2,0:T(8,128)(2,1)}, u32[]{:S(2)}) copy-start(bf16[8,128,32]{1,2,0:T(8,128)(2,1)} %copy-done.16) | copy-start | bytes 196612
  81.1 3.7 %copy-start.23 = (bf16[2,32,192]{2,1,0:T(8,128)(2,1)S(1)}, bf16[2,32,192]{2,1,0:T(8,128)(2,1)}, u32[]{:S(2)}) copy-start(bf16[2,32,192]{2,1,0:T(8,128)(2,1)} %param.12) | copy-start | bytes 73732
  81.1 4.1 %copy-start.12 = (bf16[2,128,256]{2,1,0:T(8,128)(2,1)S(1)}, bf16[2,128,256]{2,1,0:T(8,128)(2,1)}, u32[]{:S(2)}) copy-start(bf16[2,128,256]{2,1,0:T(8,128)(2,1)} %param.11) | copy-start | bytes 393220
  84.6 1.5 copy-start.1
  85.4 1.4 copy-start.31
  89.8 3.9 %copy-start.2 = (bf16[8,256,192]{1,2,0:T(8,128)(2,1)S(1)}, bf16[8,256,192]{1,2,0:T(8,128)(2,1)}, u32[]{:S(2)}) copy-start(bf16[8,256,192]{1,2,0:T(8,128)(2,1)} %copy-done.1) | copy-start | bytes 2359300
  93.2 1.3 copy-start.4
  93.2 1.3 copy-start.19
  93.3 1.3 copy-start.27
  94.5 1.9 %copy-start.28 = (f32[1,192]{1,0:T(1,128)S(1)}, f32[1,192]{1,0:T(1,128)}, u32[]{:S(2)}) copy-start(f32[1,192]{1,0:T(1,128)} %copy-done.25) | copy-start | bytes 2308
  96.4 1.7 %copy-start.15 = (bf16[8,128,32]{1,2,0:T(8,128)(2,1)S(1)}, bf16[8,128,32]{1,2,0:T(8,128)(2,1)}, u32[]{:S(2)}) copy-start(bf16[8,128,32]{1,2,0:T(8,128)(2,1)} %copy-done.14) | copy-start | bytes 196612
  96.4 2.0 %copy-start.24 = (bf16[2,32,192]{2,1,0:T(8,128)(2,1)S(1)}, bf16[2,32,192]{2,1,0:T(8,128)(2,1)}, u32[]{:S(2)}) copy-start(bf16[2,32,192]{2,1,0:T(8,128)(2,1)} %param.12) | copy-start | bytes 73732
  96.5 2.1 %copy-start.6 = (bf16[8,256,32]{1,2,0:T(8,128)(2,1)S(1)}, bf16[8,256,32]{1,2,0:T(8,128)(2,1)}, u32[]{:S(2)}) copy-start(bf16[8,256,32]{1,2,0:T(8,128)(2,1)} %copy-done.5) | copy-start | bytes 393220
  96.5 2.3 %copy-start.13 = (bf16[2,128,256]{2,1,0:T(8,128)(2,1)S(1)}, bf16[2,128,256]{2,1,0:T(8,128)(2,1)}, u32[]{:S(2)}) copy-start(bf16[2,128,256]{2,1,0:T(8,128)(2,1)} %param.11) | copy-start | bytes 393220
  99.3 1.0 copy-start.7
  100.0 0.9 copy-start.10
  100.4 2.1 %copy-start.20 = (bf16[2,256,32]{1,2,0:T(8,128)(2,1)S(1)}, bf16[2,256,32]{1,2,0:T(8,128)(2,1)}, u32[]{:S(2)}) copy-start(bf16[2,256,32]{1,2,0:T(8,128)(2,1)} %param.10) | copy-start | bytes 98308
  100.4 2.1 %copy-start.30 = (s32[256]{0:T(256)S(1)}, s32[256]{0:T(256)}, u32[]{:S(2)}) copy-start(s32[256]{0:T(256)} %param.9) | copy-start | bytes 3076
  (8 other events, 5.7 us)

commit v2 on v0

v2 whole, which is shorter than its diff:
```python
import functools

import jax
import jax.numpy as jnp
from jax import lax
from jax.experimental import pallas as pl
from jax.experimental.pallas import tpu as pltpu
from jax.sharding import PartitionSpec as P

F = 256
E = 192
MESH = pl.DeviceIdType.MESH
BF16 = jnp.bfloat16
F32 = jnp.float32
DMA = pltpu.SemaphoreType.DMA


def wrap(value, size):
    return jnp.where(value >= size, value - size, value)


class Torus:
    def __init__(self, z_lo, y, z_hi, x):
        self.z_lo, self.y, self.z_hi, self.x = z_lo, y, z_hi, x
        self.z = z_lo * z_hi
        self.flat = y * x
        self.offsets = sorted(range(y), key=lambda o: -min(o, y - o))
        self.z_steps = sorted(range(1, self.z), key=lambda o: min(o, self.z - o))

    def place(self):
        wide, grp = lax.axis_index("wide"), lax.axis_index("grp")
        z_lo = lax.div(wide, self.y)
        z_hi = lax.div(grp, 2 * self.x)
        rest = grp - z_hi * 2 * self.x
        x = lax.div(rest, 2)
        return z_hi * self.z_lo + z_lo, wide - z_lo * self.y, x, rest - 2 * x

    def split(self, z):
        high = jnp.where(z >= self.z_lo, 1, 0)
        return z - high * self.z_lo, high

    def device(self, z, y, x, core):
        z_lo, z_hi = self.split(z)
        return (z_lo * self.y + y, z_hi * 2 * self.x + x * 2 + core)


def hello(torus):
    z, y, x, core = torus.place()
    barrier = pltpu.get_barrier_semaphore()

    def signal(where):
        pl.semaphore_signal(barrier, inc=1, device_id=where, device_id_type=MESH)

    signal(torus.device(z, y, x, 1 - core))
    for step in torus.z_steps:
        signal(torus.device(wrap(z + step, torus.z), y, x, core))
    for dy in torus.offsets:
        for dx in range(torus.x):
            if dy or dx:
                signal(torus.device(z, wrap(y + dy, torus.y), wrap(x + dx, torus.x), core))


def all_here(torus):
    pl.semaphore_wait(pltpu.get_barrier_semaphore(), torus.z + torus.flat - 1)


def remote(src, dst, send, recv, where):
    return pltpu.make_async_remote_copy(
        src_ref=src, dst_ref=dst, send_sem=send, recv_sem=recv, device_id=where, device_id_type=MESH
    )


def take(ref, sem):
    pltpu.make_async_copy(ref, ref, sem).wait()


def send_z(torus, i, src, middle, z_send, z_recv):
    z, y, x, core = torus.place()
    y_to = wrap(y + torus.offsets[i], torus.y)
    z_lo, z_hi = torus.split(z)
    landing = middle.at[z_lo, z_hi, y_to]
    pltpu.make_async_copy(src.at[z_lo, y_to, z_hi], landing, z_recv.at[i]).start()
    for step in torus.z_steps:
        z_to = wrap(z + step, torus.z)
        lo_to, hi_to = torus.split(z_to)
        block = src.at[lo_to, y_to, hi_to]
        remote(block, landing, z_send, z_recv.at[i], torus.device(z_to, y, x, core)).start()


def send_flat(torus, i, middle, out, f_send, f_recv, z_recv):
    z, y, x, core = torus.place()
    y_to = wrap(y + torus.offsets[i], torus.y)
    take(middle.at[:, :, y_to], z_recv.at[i])
    for dx in range(torus.x):
        x_to = wrap(x + dx, torus.x)
        block = middle.at[:, :, y_to, x_to]
        if torus.offsets[i] == 0 and dx == 0:
            pltpu.make_async_copy(block, out(y, x), f_recv.at[i]).start()
        else:
            remote(block, out(y, x), f_send, f_recv.at[i], torus.device(z, y_to, x_to, core)).start()


NT = (((1,), (1,)), ((), ()))
TN = (((0,), (0,)), ((), ()))
NN = (((1,), (0,)), ((), ()))
K = 32
HALF = 128
ROWS = 8
ACC = 2 * HALF + 2 * K


def dot(left, right, dims):
    return lax.dot_general(left, right, dims, preferred_element_type=F32)


def read_rows(tiles, b):
    first, middle, last = (tiles[pl.ds(8 * j + b, HALF, stride=24), :] for j in range(3))
    even = jnp.concatenate([first, middle[:, :64]], axis=1)
    odd = jnp.concatenate([middle[:, 64:], last], axis=1)
    return jnp.concatenate([even, odd], axis=0).astype(BF16)


def write_rows(tiles, b, rows):
    even, odd = rows[:HALF], rows[HALF:]
    parts = (even[:, :128], jnp.concatenate([even[:, 128:], odd[:, :64]], axis=1), odd[:, 64:])
    for j, part in enumerate(parts):
        tiles[pl.ds(8 * j + b, HALF, stride=24), :] = part


PLAN = [
    "z0", "z1", "z2", "a0", "a1", "z3", "a2", "z4", "z5", "z6", "z7", "y0", "y1", "f0", "y2", "y3", "f1", "a3",
    "y4", "f2", "a4", "y5", "f3", "y6", "f4", "a5", "y7", "f5", "f6", "f7",
]


def step_kernel(
    torus,
    p_ref, cot_ref, order_ref, proj_ref, mix_ref, out_ref, lcb_ref, gain_ref,
    y_ref, d_ref, t_ref,
    pieces, inbox, src, middle, landed, spare,
    tiles, chosen, chosen_t, spread, spread_t, front, front_t, x_in, normed, inv, z_t, m_t, q_t, gq_t, gi_t, stack,
    lcb_rows, fm_rows, cot_top, cot_mid, y_rows, acc,
    leaving, middle_b, pieces_b, y_tiles, g_ref, g_spare, g_inbox, g_half, x_parts, x_own, y_parts, y_own, z_parts,
    g_done, y_full, y_dense, x_full,
    c_send, c_recv, z_send, z_recv, f_send, f_recv,
    cb_send, cb_recv, zb_send, zb_recv, fb_send, fb_recv, g_send, g_recv,
):
    z, y, x, core = torus.place()
    mate = torus.device(z, y, x, 1 - core)
    run = torus.z_hi * torus.x * 16
    block_rows = torus.z_hi * torus.x * 8
    hello(torus)

    def prepare(i):
        y_to = wrap(y + torus.offsets[i], torus.y)

        def turn(z_lo, _):
            start = pl.multiple_of((z_lo * torus.y + y_to) * run, run)
            block = p_ref[:, pl.ds(start, run)].astype(F32)
            block = jnp.concatenate([block, block], axis=0).T.astype(BF16)
            pieces[z_lo, y_to] = block.reshape(torus.z_hi, torus.x, 2, 8, 128)
            return 0

        lax.fori_loop(0, torus.z_lo, turn, 0)

    swaps = []

    def swap(i):
        y_to = wrap(y + torus.offsets[i], torus.y)
        swaps.append(remote(
            pieces.at[:, y_to, :, :, 1 - core], inbox.at[:, y_to], c_send.at[i], c_recv.at[i], mate
        ))
        swaps[i].start()

    lanes = lax.broadcasted_iota(jnp.int32, (torus.x, 8, 128), 2)
    mine = jnp.where(lanes >= 64, 1, 0) == core

    def merge(i):
        y_to = wrap(y + torus.offsets[i], torus.y)
        swaps[i].wait_recv()

        def join(z_lo, _):
            for z_hi in range(torus.z_hi):
                own = pieces[z_lo, y_to, z_hi, :, core].astype(F32)
                other = inbox[z_lo, y_to, z_hi].astype(F32)
                src[z_lo, y_to, z_hi] = jnp.where(mine, own, other).astype(BF16)
            return 0

        lax.fori_loop(0, torus.z_lo, join, 0)
        send_z(torus, i, src, middle, z_send, z_recv)

    ahead = 2
    for i in range(ahead):
        prepare(i)
    all_here(torus)
    for i in range(ahead):
        swap(i)
    for i in range(torus.y):
        if i + ahead < torus.y:
            prepare(i + ahead)
            swap(i + ahead)
        merge(i)

    spots = lax.broadcasted_iota(jnp.int32, (F, F), 0)
    places = lax.broadcasted_iota(jnp.int32, (F, F), 1)
    apart = (spots == jnp.where(places >= HALF, 2 * places - F + 1, 2 * places)).astype(F32)
    spread[...] = apart.astype(BF16)
    spread_t[...] = apart.T.astype(BF16)
    match = dot((spots == order_ref[...]).astype(BF16), spread[...], NN)
    chosen[...] = match.astype(BF16)
    chosen_t[...] = match.T.astype(BF16)
    for l in range(2):
        front[l, :HALF] = lcb_ref[l]
        front[l, HALF:] = proj_ref[l]
        front_t[l, :, :HALF] = lcb_ref[l].astype(F32).T.astype(BF16)
        front_t[l, :, HALF:] = proj_ref[l].astype(F32).T.astype(BF16)

    def open_cot(k, _):
        rows = cot_ref[pl.ds(8 * k, 8)].astype(F32).reshape(64, 128)
        tiles[pl.ds(pl.multiple_of(64 * k, 64), 64), :] = rows
        return 0

    lax.fori_loop(0, torus.z * torus.flat // 8, open_cot, 0)
    for i in range(torus.y):
        send_flat(torus, i, middle, lambda y, x: landed.at[:, y, :, x], f_send, f_recv, z_recv)
        cot_top[i] = dot(spread[...], read_rows(tiles, i), NN).astype(BF16)
    for i in range(torus.y):
        y_from = wrap(y - torus.offsets[i] + torus.y, torus.y)
        take(landed.at[:, y_from], f_recv.at[i])

        def open_rows(z_lo, _):
            start = pl.multiple_of((z_lo * torus.y + y_from) * block_rows, block_rows)
            tiles[pl.ds(start, block_rows), :] = landed[z_lo, y_from].astype(F32).reshape(block_rows, 128)
            return 0

        lax.fori_loop(0, torus.z_lo, open_rows, 0)

    for b in range(ROWS):
        x_in[0, b] = dot(chosen[...], read_rows(tiles, b), NN).astype(BF16)
    for l in range(2):
        for b in range(ROWS):
            mixed = dot(front[l], x_in[l, b], NN)
            lcb_rows[b] = mixed[:HALF]
            z_t[l, b] = mixed[HALF:].astype(BF16)
        for b in range(ROWS):
            m_t[l, K * b : K * (b + 1)] = dot(z_t[l, b], x_in[l, b], NT).astype(BF16)
        q_t[l] = dot(m_t[l], mix_ref[l], NT).astype(BF16)
        for b in range(ROWS):
            for half in range(2):
                rows = slice(half * HALF, (half + 1) * HALF)
                branch = lcb_rows[b] if half else dot(q_t[l, K * b : K * (b + 1)], out_ref[l], TN)
                summed = branch + x_in[l, b, rows].astype(F32)
                center = summed - jnp.sum(summed, axis=-1, keepdims=True) * (1.0 / E)
                variance = jnp.sum(center * center, axis=-1, keepdims=True) * (1.0 / E)
                scale = lax.rsqrt(variance + 1e-05)
                inv[l, b, rows] = scale
                value = center * scale
                normed[l, b, rows] = value
                result = (value * gain_ref[l]).astype(BF16)
                if l == 0:
                    x_in[1, b, rows] = result
                else:
                    y_rows[b, rows] = result

    pair = remote(g_ref.at[1 - core], g_inbox, g_send.at[0], g_recv.at[0], mate)
    share = g_ref.shape[2] // torus.y
    for l in (1, 0):
        gain_total = jnp.zeros((8, E), F32)
        for b in range(ROWS):
            for half in range(2):
                rows = slice(half * HALF, (half + 1) * HALF)
                cot = (cot_top if l else cot_mid)[b, rows].astype(F32)
                value = normed[l, b, rows]
                gain_total += jnp.sum((cot * value).reshape(HALF // 8, 8, E), axis=0)
                d_norm = cot * gain_ref[l]
                mean = jnp.sum(d_norm, axis=-1, keepdims=True) * (1.0 / E)
                along = jnp.sum(d_norm * value, axis=-1, keepdims=True) * (1.0 / E)
                grad = (inv[l, b, rows] * (d_norm - mean - value * along)).astype(BF16)
                if half:
                    stack[b, :HALF] = grad
                else:
                    fm_rows[b] = grad
        for b in range(ROWS):
            gq_t[K * b : K * (b + 1)] = dot(out_ref[l], fm_rows[b], NT).astype(BF16)
        gi_t[...] = dot(gq_t[...], mix_ref[l], NN).astype(BF16)
        acc[:HALF] = dot(gq_t[...], m_t[l], TN)
        out_total = jnp.zeros((K, E), F32)
        for b in range(ROWS):
            out_total += dot(q_t[l, K * b : K * (b + 1)], fm_rows[b], NN)
            stack[b, HALF:] = dot(gi_t[K * b : K * (b + 1)], x_in[l, b], NN).astype(BF16)
        front_total = jnp.zeros((HALF + K, F), F32)
        for b in range(ROWS):
            front_total += dot(stack[b], x_in[l, b], NT)
        acc[2 * HALF : 2 * HALF + K] = front_total[HALF:]
        acc[HALF : 2 * HALF] = front_total[:HALF]
        gain_row = jnp.sum(gain_total, axis=0, keepdims=True)
        acc[K + 2 * HALF :, :E] = out_total
        acc[K + 2 * HALF :, E:] = jnp.zeros((K, F - E), F32)
        for part in range(3):
            acc[K + 2 * HALF + part : K + 2 * HALF + part + 1, E:] = gain_row[:, part * 64 : (part + 1) * 64]
        for k in range(torus.x):
            depth = torus.y * share
            g_ref[l, k] = acc[k * depth : (k + 1) * depth].astype(BF16)
        if l == 0:
            pair.start()
        for b in range(ROWS):
            total = dot(front_t[l], stack[b], NN) + dot(gi_t[K * b : K * (b + 1)], z_t[l, b], TN)
            total += jnp.concatenate([fm_rows[b], stack[b, :HALF]], axis=0).astype(F32)
            total = total.astype(BF16)
            if l:
                cot_mid[b] = total
            else:
                write_rows(tiles, b, dot(chosen_t[...], total, NN))

    def leave(i):
        y_to = wrap(y + torus.offsets[i], torus.y)

        def close(z_lo, _):
            start = pl.multiple_of((z_lo * torus.y + y_to) * block_rows, block_rows)
            rows = tiles[pl.ds(start, block_rows), :].reshape(torus.z_hi, torus.x, 8, 128)
            leaving[z_lo, y_to] = rows.astype(BF16)
            return 0

        lax.fori_loop(0, torus.z_lo, close, 0)
        send_z(torus, i, leaving, middle_b, zb_send, zb_recv)

    def along_x(block, landing, k):
        pltpu.make_async_copy(block(x), landing, g_recv.at[k]).start()
        for dx in range(1, torus.x):
            x_to = wrap(x + dx, torus.x)
            remote(block(x_to), landing, g_send.at[k], g_recv.at[k], torus.device(z, y, x_to, core)).start()

    def along_y(block, landing, k):
        pltpu.make_async_copy(block(y), landing, g_recv.at[k]).start()
        for dy in range(1, torus.y):
            y_to = wrap(y + dy, torus.y)
            remote(block(y_to), landing, g_send.at[k], g_recv.at[k], torus.device(z, y_to, x, core)).start()

    def sum_pair():
        pair.wait_recv()

        def add(k, _):
            g_half[k] = (g_ref[core, k].astype(F32) + g_inbox[k].astype(F32)).astype(BF16)
            return 0

        lax.fori_loop(0, torus.x, add, 0)
        along_x(lambda x_to: g_half.at[x_to], x_parts.at[x], 1)

    def sum_x():
        take(x_parts, g_recv.at[1])
        total = jnp.sum(x_parts[...].astype(F32), axis=0)
        rest = jnp.zeros((16 - share, F), F32)
        for k in range(torus.y):
            x_own[k] = jnp.concatenate([total[k * share : (k + 1) * share], rest], axis=0).astype(BF16)
        along_y(lambda y_to: x_own.at[y_to], y_parts.at[y], 2)

    def sum_y():
        take(y_parts, g_recv.at[2])
        y_own[...] = jnp.sum(y_parts[...].astype(F32), axis=0).astype(BF16)
        landing = z_parts.at[z]
        pltpu.make_async_copy(y_own, landing, g_recv.at[3]).start()
        for step in torus.z_steps:
            where = torus.device(wrap(z + step, torus.z), y, x, core)
            remote(y_own, landing, g_send.at[3], g_recv.at[3], where).start()

    def sum_z():
        take(z_parts, g_recv.at[3])
        g_done[...] = jnp.sum(z_parts[...].astype(F32), axis=0).astype(BF16)
        along_y(lambda y_to: g_done, y_full.at[y], 4)

    def share_x():
        take(y_full, g_recv.at[4])
        y_dense[...] = jnp.concatenate(
            [y_full[k].astype(F32)[:share] for k in range(torus.y)], axis=0
        ).astype(BF16)
        along_x(lambda x_to: y_dense, x_full.at[x], 5)

    last = remote(x_full, t_ref.at[core], g_send.at[6], g_recv.at[6], mate)

    def share_pair():
        take(x_full, g_recv.at[5])
        last.start()
        t_ref[core] = x_full[...]

    parts = [sum_pair, sum_x, sum_y, sum_z, share_x, share_pair]
    for step in PLAN:
        kind, i = step[0], int(step[1:])
        if kind == "a":
            parts[i]()
        elif kind == "z":
            leave(i)
        elif kind == "y":
            write_rows(y_tiles, i, dot(spread_t[...], y_rows[i], NN))
        else:
            send_flat(torus, i, middle_b, lambda y, x: pieces_b.at[:, y, :, x, core], fb_send, fb_recv, zb_recv)

    def close_y(k, _):
        rows = y_tiles[pl.ds(pl.multiple_of(64 * k, 64), 64), :].reshape(8, 8, 128)
        y_ref[pl.ds(8 * k, 8)] = rows.astype(BF16)
        return 0

    lax.fori_loop(0, torus.z * torus.flat // 8, close_y, 0)
    swaps_b = []

    def swap_b(i):
        y_from = wrap(y - torus.offsets[i] + torus.y, torus.y)
        block = pieces_b.at[:, y_from, :, :, core]
        take(block, fb_recv.at[i])
        swaps_b.append(remote(block, block, cb_send.at[i], cb_recv.at[i], mate))
        swaps_b[i].start()

    def finish(i):
        y_from = wrap(y - torus.offsets[i] + torus.y, torus.y)
        swaps_b[i].wait_recv()

        def turn(z_lo, _):
            start = pl.multiple_of((z_lo * torus.y + y_from) * run, run)
            block = pieces_b[z_lo, y_from].astype(F32).reshape(run, 128).T
            d_ref[:, pl.ds(start, run)] = jnp.where(core == 0, block[:64], block[64:]).astype(BF16)
            return 0

        lax.fori_loop(0, torus.z_lo, turn, 0)

    for i in range(torus.y):
        swap_b(i)
        if i:
            finish(i - 1)
    finish(torus.y - 1)
    last.wait()
    for i in range(torus.y):
        swaps[i].wait_send()
        swaps_b[i].wait_send()
    pair.wait_send()
    for sem in (z_send, zb_send):
        take(spare.at[pl.ds(0, (torus.z - 1) * torus.y * torus.x)], sem)
    for sem in (f_send, fb_send):
        take(spare.at[pl.ds(0, (torus.flat - 1) * torus.z)], sem)
    take(x_parts.at[pl.ds(0, torus.x - 1)], g_send.at[1])
    take(g_spare.at[pl.ds(0, torus.y - 1)], g_send.at[2])
    take(g_spare.at[pl.ds(0, torus.z - 1)], g_send.at[3])
    take(g_spare.at[pl.ds(0, torus.y - 1)], g_send.at[4])
    take(x_full.at[pl.ds(0, torus.x - 1)], g_send.at[5])


def shards(torus, pooled, owner_order, fm_proj, fm_mix, fm_out, lcb_weight, gain, cotangent):
    chips = torus.z * torus.flat
    shape = (torus.z_lo, torus.y, torus.z_hi, torus.x, 8, 128)
    both = shape[:4] + (2, 8, 128)
    middle = (torus.z_lo, torus.z_hi, torus.y, torus.x, 8, 128)
    whole = (ROWS, F, E)
    depth = ACC // torus.x
    half = (torus.x, depth, F)
    chunk = (16, F)
    vmem = pl.BlockSpec(memory_space=pltpu.VMEM)
    spare = max((torus.z - 1) * torus.y * torus.x, (torus.flat - 1) * torus.z)
    y_tiles, d_turned, total = pl.pallas_call(
        functools.partial(step_kernel, torus),
        out_shape=(
            jax.ShapeDtypeStruct((chips, 8, 128), BF16),
            jax.ShapeDtypeStruct((64, chips * 16), BF16),
            jax.ShapeDtypeStruct((2,) + half, BF16),
        ),
        in_specs=[vmem] * 8,
        out_specs=[vmem] * 3,
        scratch_shapes=[
            pltpu.VMEM(both, BF16),
            pltpu.VMEM(shape, BF16),
            pltpu.VMEM(shape, BF16),
            pltpu.VMEM(middle, BF16),
            pltpu.VMEM(shape, BF16),
            pltpu.VMEM((spare, 8, 128), BF16),
            pltpu.VMEM((chips * 8, 128), F32),
            pltpu.VMEM((F, F), BF16),
            pltpu.VMEM((F, F), BF16),
            pltpu.VMEM((F, F), BF16),
            pltpu.VMEM((F, F), BF16),
            pltpu.VMEM((2, HALF + K, F), BF16),
            pltpu.VMEM((2, F, HALF + K), BF16),
            pltpu.VMEM((2,) + whole, BF16),
            pltpu.VMEM((2,) + whole, F32),
            pltpu.VMEM((2, ROWS, F, 1), F32),
            pltpu.VMEM((2, ROWS, K, E), BF16),
            pltpu.VMEM((2, ROWS * K, F), BF16),
            pltpu.VMEM((2, ROWS * K, HALF), BF16),
            pltpu.VMEM((ROWS * K, HALF), BF16),
            pltpu.VMEM((ROWS * K, F), BF16),
            pltpu.VMEM((ROWS, HALF + K, E), BF16),
            pltpu.VMEM((ROWS, HALF, E), F32),
            pltpu.VMEM((ROWS, HALF, E), BF16),
            pltpu.VMEM(whole, BF16),
            pltpu.VMEM(whole, BF16),
            pltpu.VMEM(whole, BF16),
            pltpu.VMEM((ACC, F), F32),
            pltpu.VMEM(shape, BF16),
            pltpu.VMEM(middle, BF16),
            pltpu.VMEM(both, BF16),
            pltpu.VMEM((chips * 8, 128), F32),
            pltpu.VMEM((2,) + half, BF16),
            pltpu.VMEM((max(torus.y, torus.z) - 1,) + chunk, BF16),
            pltpu.VMEM(half, BF16),
            pltpu.VMEM(half, BF16),
            pltpu.VMEM(half, BF16),
            pltpu.VMEM((torus.y,) + chunk, BF16),
            pltpu.VMEM((torus.y,) + chunk, BF16),
            pltpu.VMEM(chunk, BF16),
            pltpu.VMEM((torus.z,) + chunk, BF16),
            pltpu.VMEM(chunk, BF16),
            pltpu.VMEM((torus.y,) + chunk, BF16),
            pltpu.VMEM(half[1:], BF16),
            pltpu.VMEM(half, BF16),
        ]
        + [DMA((torus.y,)), DMA((torus.y,)), DMA, DMA((torus.y,)), DMA, DMA((torus.y,))] * 2
        + [DMA((7,)), DMA((7,))],
        compiler_params=pltpu.CompilerParams(
            collective_id=0, has_side_effects=True, vmem_limit_bytes=56 * 1024 * 1024
        ),
        name="train_step",
    )(
        pooled.T, cotangent.reshape(ROWS, chips, 128).transpose(1, 0, 2), owner_order.reshape(1, F),
        fm_proj.transpose(0, 2, 1), fm_mix, fm_out, lcb_weight, gain.reshape(2, 1, E),
    )
    total = total.reshape(2, -1, F).astype(F32) * (1.0 / pooled.shape[0])
    return (
        y_tiles.transpose(1, 0, 2).reshape(ROWS, F * E),
        d_turned.T,
        total[:, F : F + K].transpose(0, 2, 1),
        total[:, :HALF],
        total[:, F + K :, :E],
        total[:, HALF:F],
        total[:, F + K : F + K + 3, E:].reshape(2, E),
    )


def solution(mesh):
    torus = Torus(6, mesh.shape["wide"] // 6, 2, mesh.shape["grp"] // 4)
    return jax.shard_map(
        functools.partial(shards, torus),
        mesh=mesh,
        in_specs=(P(None, ("wide", "grp")), P(), P(), P(), P(), P(), P(), P(("wide", "grp"), None)),
        out_specs=(P(("wide", "grp"), None), P(None, ("wide", "grp")), P(), P(), P(), P(), P()),
        check_vma=False,
    )
```

time: 698 us -> 119 us (0.17)
  waiting for transfers between devices: 411 us -> 0 us
  blocking collectives: 149 us -> 0 us
  Pallas kernels: 0 us -> 110 us
  starting transfers between devices: 48.1 us -> 0 us
  local copies, waits for them, and re-layouts: 48.4 us -> 6.38 us
  between operations: 14.7 us -> 0.67 us
  other arithmetic: 14.7 us -> 1.03 us
  matrix products: 11.1 us -> 0 us
    psum x1 -> x0, waiting for transfers between devices: 364 us -> none  [shards(): totals = lax.psum(grads, ('wide', 'grp'))]
    psum x1 -> x0, blocking collectives: 111 us -> none  [shards(): totals = lax.psum(grads, ('wide', 'grp'))]
    pallas_call x0 -> x1, Pallas kernels: none -> 110 us  [shards(): pl.pallas_call(functools.partial(step_kernel, torus), out_shape=(jax.Shap...]
    all_to_all x3 -> x0, starting transfers between devices: 48.1 us -> none  [the longest x1 28.2 us: shards(): lax.all_to_all(sectioned, 'wide', split_axis=0, concat_axis=1, tiled=True)]
    all_to_all x3 -> x0, waiting for transfers between devices: 46.7 us -> none  [the longest x1 23.7 us: shards(): lax.all_to_all(back_rows, 'wide', split_axis=1, concat_axis=0, tiled=True)]
    all_to_all x1 -> x0, blocking collectives: 38.3 us -> none  [shards(): lax.all_to_all(arranged, 'grp', split_axis=0, concat_axis=1, tiled=True)]
    all_to_all x9 -> x0, local copies, waits for them, and re-layouts: 17.8 us -> none  [the longest x3 6.8 us: shards(): lax.all_to_all(across, 'grp', split_axis=1, concat_axis=0, tiled=True)]
    dot_general x30 -> x0, matrix products: 11.1 us -> none  [product(): return jnp.einsum(form, left, right, preferred_element_type=jnp.float32)]
  transfers between devices with their start and end apart: 4 -> 0, of which waited for: 3 -> 0; matrix products, arithmetic and copies ran while one was open for 3% -> 0% of each run, Pallas kernels for 0% -> 0%
where the time goes in v2:
time: 119 us
  Pallas kernels  110 us (92%)
  local copies, waits for them, and re-layouts  6.38 us (5%)
    pallas_call x1, Pallas kernels, shards(): pl.pallas_call(functools.partial(step_kernel, torus), out_shape=(jax.Shap...  110 us
    unnamed x8, local copies, waits for them, and re-layouts  2.97 us

profile of v2, /device:TPU:1, one launch (start us, length us, event | category | flops | bytes accessed | tf_op | source)
XLA Modules:
  0.0 118.5 jit_solution(2889311737986142116)
XLA Ops:
  0.6 0.0 copy-start.2
  0.6 0.7 copy-done.2
  1.3 0.6 reshape.35.gain_ref
  1.9 110.4 %train_step.1 = (bf16[384,8,128]{2,1,0:T(8,128)(2,1)}, bf16[64,6144]{1,0:T(8,128)(2,1)}, bf16[2,4,80,256]{3,2,1,0:T(8,128)(2,1)}) custom-call(bf16[64,6144]{1,0:T(8,128)(2,1)} %bitcast.19, bf16[384,8,128]{2,1,0:T(8,128)(2,1)} %bitcast.20, s32[1,256]{1,0:T(1,128)} %bitcast.22, bf16[2,32,256]{2,1,0:T(8,128)(2,1)} %bitcast.21, bf16[2,128,256]{2,1,0:T(8,128)(2,1)} %mix_ref.1, ...), custom_call_target="tpu_custom_call" | custom-call | tf_op jit(solution)/shard_map/train_step/pallas_call | solution.py:456
  112.3 1.0 convert_multiply_fusion
  113.4 0.0 copy-start.1
  113.4 0.1 slice.24
  113.4 0.7 reshape.37
  114.1 0.6 slice.22
  114.7 0.6 slice_bitcast_fusion
  115.4 0.8 fusion
  116.2 0.0 copy-done.1
  116.2 0.0 copy-start
  116.2 0.9 copy.17
  117.1 0.5 copy-done
  117.6 0.9 copy.18
Async XLA Ops:
  0.6 0.7 copy-start.2
  113.4 2.8 %copy-start.1 = (bf16[384,8,128]{2,1,0:T(8,128)(2,1)S(1)}, bf16[384,8,128]{2,1,0:T(8,128)(2,1)}, u32[]{:S(2)}) copy-start(bf16[384,8,128]{2,1,0:T(8,128)(2,1)} %get-tuple-element.10) | copy-start | bytes 2359300
  116.2 1.4 %copy-start = (bf16[64,6144]{1,0:T(8,128)(2,1)S(1)}, bf16[64,6144]{1,0:T(8,128)(2,1)}, u32[]{:S(2)}) copy-start(bf16[64,6144]{1,0:T(8,128)(2,1)} %get-tuple-element.11) | copy-start | bytes 2359300

commit v3 on v2

--- a/solution.py
+++ b/solution.py
@@ -128,27 +128,33 @@
 
 
 PLAN = [
-    "z0", "z1", "z2", "a0", "a1", "z3", "a2", "z4", "z5", "z6", "z7", "y0", "y1", "f0", "y2", "y3", "f1", "a3",
-    "y4", "f2", "a4", "y5", "f3", "y6", "f4", "a5", "y7", "f5", "f6", "f7",
+    "z0", "z1", "z2", "a0", "a1", "a2", "z3", "z4", "z5", "z6", "z7", "f0", "f1", "f2", "y0", "y1", "a3", "y2", "y3",
+    "f3", "y4", "a4", "y5", "f4", "f5", "a5", "y6", "f6", "y7", "f7",
 ]
 
 
 def step_kernel(
     torus,
-    p_ref, cot_ref, order_ref, proj_ref, mix_ref, out_ref, lcb_ref, gain_ref,
-    y_ref, d_ref, t_ref,
+    p_far, cot_far, order_far, proj_far, mix_far, out_far, lcb_far, gain_far,
+    y_ref, d_ref, proj_sum, mix_sum, out_sum, lcb_sum, gain_sum,
+    p_ref, cot_ref, order_ref, proj_ref, mix_ref, out_ref, lcb_ref, gain_ref, t_ref,
     pieces, inbox, src, middle, landed, spare,
     tiles, chosen, chosen_t, spread, spread_t, front, front_t, x_in, normed, inv, z_t, m_t, q_t, gq_t, gi_t, stack,
     lcb_rows, fm_rows, cot_top, cot_mid, y_rows, acc,
     leaving, middle_b, pieces_b, y_tiles, g_ref, g_spare, g_inbox, g_half, x_parts, x_own, y_parts, y_own, z_parts,
     g_done, y_full, y_dense, x_full,
     c_send, c_recv, z_send, z_recv, f_send, f_recv,
-    cb_send, cb_recv, zb_send, zb_recv, fb_send, fb_recv, g_send, g_recv,
+    cb_send, cb_recv, zb_send, zb_recv, fb_send, fb_recv, g_send, g_recv, near,
 ):
     z, y, x, core = torus.place()
     mate = torus.device(z, y, x, 1 - core)
     run = torus.z_hi * torus.x * 16
     block_rows = torus.z_hi * torus.x * 8
+    far = (p_far, cot_far, order_far, proj_far, mix_far, out_far, lcb_far, gain_far)
+    here = (p_ref, cot_ref, order_ref, proj_ref, mix_ref, out_ref, lcb_ref, gain_ref)
+    loads = [pltpu.make_async_copy(a, b, near.at[k]) for k, (a, b) in enumerate(zip(far, here))]
+    for load in loads:
+        load.start()
     hello(torus)
 
     def prepare(i):
@@ -189,18 +195,20 @@
         lax.fori_loop(0, torus.z_lo, join, 0)
         send_z(torus, i, src, middle, z_send, z_recv)
 
-    ahead = 2
-    for i in range(ahead):
-        prepare(i)
+    loads[0].wait()
+    prepare(0)
     all_here(torus)
-    for i in range(ahead):
-        swap(i)
+    swap(0)
+    prepare(1)
+    swap(1)
     for i in range(torus.y):
-        if i + ahead < torus.y:
-            prepare(i + ahead)
-            swap(i + ahead)
         merge(i)
-
+        if i + 2 < torus.y:
+            prepare(i + 2)
+            swap(i + 2)
+
+    for load in loads[1:]:
+        load.wait()
     spots = lax.broadcasted_iota(jnp.int32, (F, F), 0)
     places = lax.broadcasted_iota(jnp.int32, (F, F), 1)
     apart = (spots == jnp.where(places >= HALF, 2 * places - F + 1, 2 * places)).astype(F32)
@@ -256,7 +264,7 @@
                 inv[l, b, rows] = scale
                 value = center * scale
                 normed[l, b, rows] = value
-                result = (value * gain_ref[l]).astype(BF16)
+                result = (value * gain_ref[l : l + 1]).astype(BF16)
                 if l == 0:
                     x_in[1, b, rows] = result
                 else:
@@ -272,7 +280,7 @@
                 cot = (cot_top if l else cot_mid)[b, rows].astype(F32)
                 value = normed[l, b, rows]
                 gain_total += jnp.sum((cot * value).reshape(HALF // 8, 8, E), axis=0)
-                d_norm = cot * gain_ref[l]
+                d_norm = cot * gain_ref[l : l + 1]
                 mean = jnp.sum(d_norm, axis=-1, keepdims=True) * (1.0 / E)
                 along = jnp.sum(d_norm * value, axis=-1, keepdims=True) * (1.0 / E)
                 grad = (inv[l, b, rows] * (d_norm - mean - value * along)).astype(BF16)
@@ -306,11 +314,9 @@
         for b in range(ROWS):
             total = dot(front_t[l], stack[b], NN) + dot(gi_t[K * b : K * (b + 1)], z_t[l, b], TN)
             total += jnp.concatenate([fm_rows[b], stack[b, :HALF]], axis=0).astype(F32)
-            total = total.astype(BF16)
-            if l:
-                cot_mid[b] = total
-            else:
-                write_rows(tiles, b, dot(chosen_t[...], total, NN))
+            cot_mid[b] = total.astype(BF16)
+    for b in range(ROWS):
+        write_rows(tiles, b, dot(chosen_t[...], cot_mid[b], NN))
 
     def leave(i):
         y_to = wrap(y + torus.offsets[i], torus.y)
@@ -421,12 +427,23 @@
 
         lax.fori_loop(0, torus.z_lo, turn, 0)
 
-    for i in range(torus.y):
+    for i in range(torus.y - 1):
         swap_b(i)
         if i:
             finish(i - 1)
+    last.wait_recv()
+    scale = 1.0 / (torus.z * torus.flat * 16)
+    for l in range(2):
+        total = t_ref[l].astype(F32).reshape(ACC, F) * scale
+        mix_sum[l] = total[:HALF]
+        lcb_sum[l] = total[HALF:F]
+        proj_sum[l] = total[F : F + K]
+        out_sum[l] = total[F + K :, :E]
+        gain_sum[l : l + 1] = jnp.concatenate([total[F + K + k : F + K + k + 1, E:] for k in range(3)], axis=1)
+    finish(torus.y - 2)
+    swap_b(torus.y - 1)
     finish(torus.y - 1)
-    last.wait()
+    last.wait_send()
     for i in range(torus.y):
         swaps[i].wait_send()
         swaps_b[i].wait_send()
@@ -453,16 +470,26 @@
     chunk = (16, F)
     vmem = pl.BlockSpec(memory_space=pltpu.VMEM)
     spare = max((torus.z - 1) * torus.y * torus.x, (torus.flat - 1) * torus.z)
-    y_tiles, d_turned, total = pl.pallas_call(
+    operands = (
+        pooled.T, cotangent.reshape(ROWS, chips, 128).transpose(1, 0, 2), owner_order.reshape(1, F),
+        fm_proj.transpose(0, 2, 1), fm_mix, fm_out, lcb_weight, gain,
+    )
+    y_tiles, d_turned, proj_sum, mix_sum, out_sum, lcb_sum, gain_sum = pl.pallas_call(
         functools.partial(step_kernel, torus),
         out_shape=(
             jax.ShapeDtypeStruct((chips, 8, 128), BF16),
             jax.ShapeDtypeStruct((64, chips * 16), BF16),
-            jax.ShapeDtypeStruct((2,) + half, BF16),
+            jax.ShapeDtypeStruct((2, K, F), F32),
+            jax.ShapeDtypeStruct((2, HALF, F), F32),
+            jax.ShapeDtypeStruct((2, K, E), F32),
+            jax.ShapeDtypeStruct((2, HALF, F), F32),
+            jax.ShapeDtypeStruct((2, E), F32),
         ),
-        in_specs=[vmem] * 8,
-        out_specs=[vmem] * 3,
-        scratch_shapes=[
+        in_specs=[pl.BlockSpec(memory_space=pl.ANY)] * 8,
+        out_specs=[vmem] * 7,
+        scratch_shapes=[pltpu.VMEM(a.shape, a.dtype) for a in operands]
+        + [
+            pltpu.VMEM((2,) + half, BF16),
             pltpu.VMEM(both, BF16),
             pltpu.VMEM(shape, BF16),
             pltpu.VMEM(shape, BF16),
@@ -510,24 +537,20 @@
             pltpu.VMEM(half, BF16),
         ]
         + [DMA((torus.y,)), DMA((torus.y,)), DMA, DMA((torus.y,)), DMA, DMA((torus.y,))] * 2
-        + [DMA((7,)), DMA((7,))],
+        + [DMA((7,)), DMA((7,)), DMA((8,))],
         compiler_params=pltpu.CompilerParams(
             collective_id=0, has_side_effects=True, vmem_limit_bytes=56 * 1024 * 1024
         ),
         name="train_step",
-    )(
-        pooled.T, cotangent.reshape(ROWS, chips, 128).transpose(1, 0, 2), owner_order.reshape(1, F),
-        fm_proj.transpose(0, 2, 1), fm_mix, fm_out, lcb_weight, gain.reshape(2, 1, E),
-    )
-    total = total.reshape(2, -1, F).astype(F32) * (1.0 / pooled.shape[0])
+    )(*operands)
     return (
         y_tiles.transpose(1, 0, 2).reshape(ROWS, F * E),
         d_turned.T,
-        total[:, F : F + K].transpose(0, 2, 1),
-        total[:, :HALF],
-        total[:, F + K :, :E],
-        total[:, HALF:F],
-        total[:, F + K : F + K + 3, E:].reshape(2, E),
+        proj_sum.transpose(0, 2, 1),
+        mix_sum,
+        out_sum,
+        lcb_sum,
+        gain_sum,
     )
 
 

time: 119 us -> 114 us (0.958)
  Pallas kernels: 110 us -> 107 us
    unnamed x8 -> x19, local copies, waits for them, and re-layouts: 2.97 us -> 6.43 us
    pallas_call x1, Pallas kernels: 110 us -> 107 us  [shards(): pl.pallas_call(functools.partial(step_kernel, torus), out_shape=(jax.Shap...]
    slice x3 -> x0, local copies, waits for them, and re-layouts: 1.53 us -> none  [the longest x1 0.83 us: shards(): total[:, HALF:F]]
    reshape x2 -> x0, local copies, waits for them, and re-layouts: 1.24 us -> none  [the longest x1 0.66 us: shards(): total[:, F + K:F + K + 3, E:].reshape(2, E)]
where the time goes in v3:
time: 114 us
  Pallas kernels  107 us (94%)
  local copies, waits for them, and re-layouts  6.43 us (6%)
    pallas_call x1, Pallas kernels, shards(): pl.pallas_call(functools.partial(step_kernel, torus), out_shape=(jax.Shap...  107 us
    unnamed x19, local copies, waits for them, and re-layouts  6.43 us

profile of v3, /device:TPU:1, one launch (start us, length us, event | category | flops | bytes accessed | tf_op | source)
XLA Modules:
  0.0 114.1 jit_solution(15975284569629871988)
XLA Ops:
  0.6 107.0 %train_step.1 = (bf16[384,8,128]{2,1,0:T(8,128)(2,1)}, bf16[64,6144]{1,0:T(8,128)(2,1)}, f32[2,32,256]{2,1,0:T(8,128)}, f32[2,128,256]{2,1,0:T(8,128)}, f32[2,32...) custom-call(bf16[64,6144]{1,0:T(8,128)(2,1)} %bitcast.13, bf16[384,8,128]{2,1,0:T(8,128)(2,1)} %bitcast.14, ...), custom_call_target="tpu_custom_call" | custom-call | tf_op jit(solution)/shard_map/train_step/pallas_call | solution.py:477
  107.7 0.0 copy-start
  107.7 2.1 %copy.22 = bf16[8,49152]{1,0:T(8,128)(2,1)} copy(bf16[8,49152]{1,0:T(8,128)(2,1)} %bitcast.12) | data formatting | bytes 1572864
  109.8 0.0 copy-done
  109.8 0.0 copy-start.4
  109.8 0.0 copy-start.2
  109.8 0.9 copy.23
  110.7 0.0 copy-done.4
  110.7 0.6 copy.24
  111.3 0.0 copy-done.2
  111.3 0.0 copy-start.3
  111.4 0.0 copy-start.1
  111.4 0.7 copy.25
  112.1 0.2 copy-done.3
  112.2 0.6 copy.26
  112.8 0.0 copy-done.1
  112.8 0.0 copy-start.5
  112.8 0.7 copy.27
  113.6 0.0 copy-done.5
  113.6 0.6 copy.28
Async XLA Ops:
  107.7 2.1 %copy-start = (bf16[64,6144]{1,0:T(8,128)(2,1)S(1)}, bf16[64,6144]{1,0:T(8,128)(2,1)}, u32[]{:S(2)}) copy-start(bf16[64,6144]{1,0:T(8,128)(2,1)} %get-tuple-element.15) | copy-start | bytes 2359300
  109.8 0.9 copy-start.4
  109.8 1.5 %copy-start.2 = (f32[2,128,256]{2,1,0:T(8,128)S(1)}, f32[2,128,256]{2,1,0:T(8,128)}, u32[]{:S(2)}) copy-start(f32[2,128,256]{2,1,0:T(8,128)} %get-tuple-element.31) | copy-start | bytes 786436
  111.3 0.9 copy-start.3
  111.4 1.5 %copy-start.1 = (f32[2,128,256]{2,1,0:T(8,128)S(1)}, f32[2,128,256]{2,1,0:T(8,128)}, u32[]{:S(2)}) copy-start(f32[2,128,256]{2,1,0:T(8,128)} %get-tuple-element.33) | copy-start | bytes 786436
  112.8 0.7 copy-start.5

commit v4 on v3

--- a/solution.py
+++ b/solution.py
@@ -195,6 +195,9 @@
         lax.fori_loop(0, torus.z_lo, join, 0)
         send_z(torus, i, src, middle, z_send, z_recv)
 
+    def onward(i):
+        send_flat(torus, i, middle, lambda y, x: landed.at[:, y, :, x], f_send, f_recv, z_recv)
+
     loads[0].wait()
     prepare(0)
     all_here(torus)
@@ -206,6 +209,8 @@
         if i + 2 < torus.y:
             prepare(i + 2)
             swap(i + 2)
+        else:
+            onward(i + 2 - torus.y)
 
     for load in loads[1:]:
         load.wait()
@@ -230,7 +235,8 @@
 
     lax.fori_loop(0, torus.z * torus.flat // 8, open_cot, 0)
     for i in range(torus.y):
-        send_flat(torus, i, middle, lambda y, x: landed.at[:, y, :, x], f_send, f_recv, z_recv)
+        if i >= 2:
+            onward(i)
         cot_top[i] = dot(spread[...], read_rows(tiles, i), NN).astype(BF16)
     for i in range(torus.y):
         y_from = wrap(y - torus.offsets[i] + torus.y, torus.y)
@@ -459,6 +465,35 @@
     take(x_full.at[pl.ds(0, torus.x - 1)], g_send.at[5])
 
 
+def hand_over_kernel(*refs):
+    count = len(refs) // 2
+    sems = refs[-1]
+    copies = []
+    for source, target in zip(refs[:count], refs[count : 2 * count]):
+        pieces = 4 if source.dtype == BF16 else 1
+        size = source.shape[0] // pieces
+        for k in range(pieces):
+            rows = pl.ds(k * size, size)
+            copies.append(pltpu.make_async_copy(source.at[rows], target.at[rows], sems.at[len(copies)]))
+    for copy in copies:
+        copy.start()
+    for copy in copies:
+        copy.wait()
+
+
+def hand_over(arrays):
+    anywhere = pl.BlockSpec(memory_space=pl.ANY)
+    return pl.pallas_call(
+        hand_over_kernel,
+        out_shape=tuple(jax.ShapeDtypeStruct(a.shape, a.dtype) for a in arrays),
+        in_specs=[anywhere] * len(arrays),
+        out_specs=[anywhere] * len(arrays),
+        scratch_shapes=[DMA((4 * len(arrays),))],
+        compiler_params=pltpu.CompilerParams(vmem_limit_bytes=56 * 1024 * 1024),
+        name="hand_over",
+    )(*arrays)
+
+
 def shards(torus, pooled, owner_order, fm_proj, fm_mix, fm_out, lcb_weight, gain, cotangent):
     chips = torus.z * torus.flat
     shape = (torus.z_lo, torus.y, torus.z_hi, torus.x, 8, 128)
@@ -474,7 +509,7 @@
         pooled.T, cotangent.reshape(ROWS, chips, 128).transpose(1, 0, 2), owner_order.reshape(1, F),
         fm_proj.transpose(0, 2, 1), fm_mix, fm_out, lcb_weight, gain,
     )
-    y_tiles, d_turned, proj_sum, mix_sum, out_sum, lcb_sum, gain_sum = pl.pallas_call(
+    results = pl.pallas_call(
         functools.partial(step_kernel, torus),
         out_shape=(
             jax.ShapeDtypeStruct((chips, 8, 128), BF16),
@@ -543,6 +578,7 @@
         ),
         name="train_step",
     )(*operands)
+    y_tiles, d_turned, proj_sum, mix_sum, out_sum, lcb_sum, gain_sum = hand_over(results)
     return (
         y_tiles.transpose(1, 0, 2).reshape(ROWS, F * E),
         d_turned.T,

time: 114 us -> 177 us (1.55)
  Pallas kernels: 107 us -> 176 us
  local copies, waits for them, and re-layouts: 6.43 us -> 0 us
    pallas_call x0 -> x1, Pallas kernels: none -> 68.9 us  [hand_over(): pl.pallas_call(hand_over_kernel, out_shape=tuple((jax.ShapeDtypeStruct(a....]
    unnamed x19 -> x0, local copies, waits for them, and re-layouts: 6.43 us -> none
where the time goes in v4:
time: 177 us
  Pallas kernels  176 us (99%)
    pallas_call x1, Pallas kernels, shards(): pl.pallas_call(functools.partial(step_kernel, torus), out_shape=(jax.Shap...  107 us
    pallas_call x1, Pallas kernels, hand_over(): pl.pallas_call(hand_over_kernel, out_shape=tuple((jax.ShapeDtypeStruct(a....  68.9 us

profile of v4, /device:TPU:1, one launch (start us, length us, event | category | flops | bytes accessed | tf_op | source)
XLA Modules:
  0.0 176.6 jit_solution(2531260464889921079)
XLA Ops:
  0.6 107.0 %train_step.1 = (bf16[384,8,128]{2,1,0:T(8,128)(2,1)}, bf16[64,6144]{1,0:T(8,128)(2,1)}, f32[2,32,256]{2,1,0:T(8,128)}, f32[2,128,256]{2,1,0:T(8,128)}, f32[2,32...) custom-call(bf16[64,6144]{1,0:T(8,128)(2,1)} %bitcast.11, bf16[384,8,128]{2,1,0:T(8,128)(2,1)} %bitcast.12, ...), custom_call_target="tpu_custom_call" | custom-call | tf_op jit(solution)/shard_map/train_step/pallas_call | solution.py:512
  107.7 68.9 %hand_over.1 = (bf16[384,8,128]{2,1,0:T(8,128)(2,1)}, bf16[64,6144]{1,0:T(8,128)(2,1)}, f32[2,32,256]{2,1,0:T(8,128)}, f32[2,128,256]{2,1,0:T(8,128)}, f32[2,32,...) custom-call(bf16[384,8,128]{2,1,0:T(8,128)(2,1)} %get-tuple-element.21.refs_0_, ...), custom_call_target="tpu_custom_call" | custom-call | tf_op jit(solution)/shard_map/hand_over/pallas_call | solution.py:486
